TPU v7x, 128 devices: a whole 4x4x4 slice. The times are simulated.
128 devices in a mesh: gx: 8 (over z, core), gy: 16 (over y, x).
Axes of the slice: x: 4, y: 4, z: 4, core: 2. Of those that a mesh axis runs over, the one named last changes fastest.
Arguments:
- irreps: bfloat16 [8, 16, 128, 25, 128], P('gx', 'gy'), may hold values from -6 to 6
- mix_weight: bfloat16 [5, 128, 128], replicated, may hold values from -0.5 to 0.5
- readout: bfloat16 [25, 128], replicated, may hold values from -0.5 to 0.5
- ghost_x: int32 [8, 16, 2, 64], P('gx', 'gy'), may hold values from 0 to 127
- ghost_y: int32 [8, 16, 2, 64], P('gx', 'gy'), may hold values from 0 to 255
- edge_source_row: int32 [8, 16, 2048], P('gx', 'gy'), may hold values from 0 to 383
- edge_dst: int32 [8, 16, 2048], P('gx', 'gy'), may hold values from 0 to 128
- radial: float32 [8, 16, 25, 2048], P('gx', 'gy'), may hold values from -4 to 4
- tile_peer: int32 [8, 16, 32, 4], P('gx', 'gy'), may hold values from 0 to 127, all different within a row; in each aligned block of 32 rows (0 to 31, 32 to 63, ..., all dimensions but the last counted through in order) at most 2 rows name the same one
- tile_block: int32 [8, 16, 32, 4], P('gx', 'gy'), may hold values from 0 to 15
- tile_count: int32 [8, 16, 32], P('gx', 'gy'), may hold values from 1 to 4
- basis: bfloat16 [8, 16, 32, 200, 256], P('gx', 'gy'), may hold values from -0.21875 to 0.21875
- density_cot: bfloat16 [8, 16, 2048], P('gx', 'gy'), may hold values from -6 to 6
Outputs:
- density: float32 [8, 16, 2048], P('gx', 'gy')
- grad_weights: float32 [5, 128, 128], replicated
Inputs may be any that keep to these rules, and one draw needn't show every extreme that they name: `tile_peer`: among the 32 x 4 slots of one pencil, used or not, no brick is named more than 2 times, a bound that some block reaches; the slots of one tile name different bricks. `edge_dst`: an edge slot whose destination is 128 is padding.
All inputs are finite; a program needn't handle non-finite values.
Results may differ from a plain program's by a relative error of at most 0.014.
Values may be sent and summed in bfloat16 or wider, within the bound.
A program may use at most 192 MiB of HBM per device.

v0:
```python
import functools

import jax
import jax.numpy as jnp
from jax import lax
from jax.experimental import pallas as pl
from jax.experimental.pallas import tpu as pltpu
from jax.sharding import PartitionSpec as P

MESH = pl.DeviceIdType.MESH
BF = jnp.bfloat16
F32 = jnp.float32

CHUNKS = ((0, 4), (16, 21), (21, 25), (9, 13), (13, 16), (4, 9))
DEGREES = 5


def degree_of(m):
    l = 0
    while (l + 1) * (l + 1) <= m:
        l += 1
    return l


def iota(shape, dim):
    return lax.broadcasted_iota(jnp.int32, shape, dim)


def dot(a, b):
    return jnp.dot(a, b, preferred_element_type=F32)


def dot_nt(a, b):
    return lax.dot_general(a, b, (((1,), (1,)), ((), ())), preferred_element_type=F32)


def dot_tn(a, b):
    return lax.dot_general(a, b, (((0,), (0,)), ((), ())), preferred_element_type=F32)


def kernel(
    nx, ny,
    irr, w, ro, small, src, dst, rad, cot, basis_hbm,
    dens_out, gw_out,
    basis, ghost, xface, yface, hot_x, hot_y, source_hot, dst_mask, scaled, op,
    y_st, g_st, gg_st, gate, coef, gate_grad, atom_grad, tmp256,
    s_a, r_a, s_b, r_b, s_c, r_c, s_d, r_d, pick_p, own_hot, dens,
    gw_send, gw_recv, sum_x_send, sum_x, sum_y, out_recv,
    basis_sem, xs_sem, xr_sem, ys_sem, yr_sem,
    as_sem, ar_sem, bs_sem, br_sem, cs_sem, cr_sem, ds_sem, dr_sem,
    ws_sem, wr_sem, us_sem, ur_sem, vs_sem, vr_sem, os_sem, or_sem,
):
    ix = lax.axis_index("gx")
    iy = lax.axis_index("gy")
    yq, yr = iy // 4, iy % 4
    left, right = (ix + nx - 1) % nx, (ix + 1) % nx
    lower, upper = (iy + ny - 1) % ny, (iy + 1) % ny

    basis_copy = pltpu.make_async_copy(basis_hbm, basis, basis_sem)
    basis_copy.start()

    barrier = pltpu.get_barrier_semaphore()

    def greet_x(d, c):
        pl.semaphore_signal(barrier, inc=1, device_id=((ix + d) % nx, iy), device_id_type=MESH)
        return c

    def greet_y(d, c):
        pl.semaphore_signal(barrier, inc=1, device_id=(ix, (iy + d) % ny), device_id_type=MESH)
        return c

    lax.fori_loop(1, nx, greet_x, 0)
    lax.fori_loop(1, ny, greet_y, 0)

    def remote(s, d, ssem, rsem, i, j):
        return pltpu.make_async_remote_copy(
            src_ref=s, dst_ref=d, send_sem=ssem, recv_sem=rsem, device_id=(i, j), device_id_type=MESH
        )

    def x_copies(c):
        lo, hi = CHUNKS[c]
        n = hi - lo
        return (
            remote(xface.at[pl.ds(lo, n), pl.ds(64, 64), :], ghost.at[pl.ds(lo, n), pl.ds(0, 64), :],
                   xs_sem.at[c, 0], xr_sem.at[c, 0], right, iy),
            remote(xface.at[pl.ds(lo, n), pl.ds(0, 64), :], ghost.at[pl.ds(lo, n), pl.ds(64, 64), :],
                   xs_sem.at[c, 1], xr_sem.at[c, 1], left, iy),
        )

    def y_copies(c):
        lo, hi = CHUNKS[c]
        n = hi - lo
        return (
            remote(yface.at[pl.ds(lo, n), pl.ds(64, 64), :], ghost.at[pl.ds(lo, n), pl.ds(128, 64), :],
                   ys_sem.at[c, 0], yr_sem.at[c, 0], ix, upper),
            remote(yface.at[pl.ds(lo, n), pl.ds(0, 64), :], ghost.at[pl.ds(lo, n), pl.ds(192, 64), :],
                   ys_sem.at[c, 1], yr_sem.at[c, 1], ix, lower),
        )

    sm = small[...]
    hot_x[...] = jnp.where(iota((128, 128), 0) == sm[0:1, :], 1.0, 0.0).T.astype(BF)

    def send_x(c):
        lo, hi = CHUNKS[c]
        chooser = hot_x[...]
        for m in range(lo, hi):
            xface[m] = dot(chooser, irr[m]).astype(BF)
        if c == 0:
            pl.semaphore_wait(barrier, nx + ny - 2)
        for copy in x_copies(c):
            copy.start()

    for c in range(len(CHUNKS)):
        send_x(c)

    for half in range(2):
        hot_y[:, half * 128:(half + 1) * 128] = (
            jnp.where(iota((128, 128), 0) + half * 128 == sm[1:2, :], 1.0, 0.0).T.astype(BF)
        )

    def send_y(c):
        for copy in x_copies(c):
            copy.wait_recv()
        lo, hi = CHUNKS[c]
        for m in range(lo, hi):
            rows = dot(hot_y[:, 0:128], irr[m]) + dot(hot_y[:, 128:256], ghost[m, 0:128, :])
            yface[m] = rows.astype(BF)
        for copy in y_copies(c):
            copy.start()

    src_cols = jnp.concatenate([src[...].astype(F32), jnp.zeros((112, 128), F32)], axis=0).T
    lane384 = iota((128, 384), 1).astype(F32)
    sub128 = iota((128, 128), 0)
    for k in range(16):
        source_hot[k * 128:(k + 1) * 128, :] = jnp.where(src_cols[:, k:k + 1] == lane384, 1.0, 0.0).astype(BF)
        dst_mask[:, k * 128:(k + 1) * 128] = jnp.where(sub128 == dst[k:k + 1, :], 1.0, 0.0).astype(BF)

    def build_op(c):
        lo, hi = CHUNKS[c]
        n = hi - lo
        for i in range(n):
            row = rad[lo + i].astype(BF)
            scaled[i * 128:(i + 1) * 128, :] = dst_mask[...] * jnp.broadcast_to(row, (128, 2048))
        built = dot(scaled[0:n * 128, :], source_hot[...])
        for i in range(n):
            op[lo + i] = built[i * 128:(i + 1) * 128, :].astype(BF)

    send_y(0)
    build_op(0)

    peer_row = sm[2:3, :]
    same = (jnp.broadcast_to(peer_row, (128, 128)).astype(F32).T == peer_row.astype(F32)) & (
        iota((128, 128), 0) < iota((128, 128), 1)
    )
    rank = jnp.sum(jnp.where(same, 1.0, 0.0), axis=0, keepdims=True).astype(jnp.int32)
    live_row = (iota((1, 128), 1) % 4) < sm[4:5, :]
    position = jnp.where(live_row, peer_row * 2 + rank, -1)
    chosen = jnp.where(iota((256, 128), 0) == position, 1.0, 0.0)
    for half in range(2):
        pick_p[:, half * 128:(half + 1) * 128] = chosen[half * 128:(half + 1) * 128, :].T.astype(BF)
    spread = jnp.where(iota((128, 16), 1) == iota((128, 16), 0) // 8, 1.0, 0.0).astype(BF)
    picked = dot(spread, cot[...])
    rolled = pltpu.roll(picked, 64, 1)
    odd = (iota((128, 128), 0) // 4) % 2
    mine = jnp.where((iota((128, 128), 1) // 64) == odd, picked, rolled)
    both = jnp.concatenate([mine, mine], axis=1)
    weights = jnp.where(iota((128, 256), 1) // 64 == iota((128, 256), 0) % 4, both, 0.0).astype(BF)

    send_y(1)
    basis_copy.wait()

    lane_tile = iota((200, 128), 1) // 4

    def slot_step(t, acc):
        return jnp.where(lane_tile == t, dot_nt(basis[t], weights), acc)

    slot_grad = lax.fori_loop(0, 32, slot_step, jnp.zeros((200, 128), F32))
    id_rows = jnp.where(iota((56, 128), 0) == 0, jnp.broadcast_to(sm[3:4, :].astype(F32), (56, 128)), 0.0)
    tmp256[...] = jnp.concatenate([slot_grad, id_rows], axis=0)
    sent = dot_nt(chosen.astype(BF), tmp256[...].astype(BF)).astype(BF)
    for k in range(nx):
        s_a[k] = sent[k * 32:(k + 1) * 32, :]
    r_a[ix] = s_a[ix]

    def exchange(axis, n, s, r, ssem, rsem, start):
        me = ix if axis == "x" else iy

        def step(d, c):
            other = (me + d) % n
            to = (other, iy) if axis == "x" else (ix, other)
            if start == "recv":
                remote(s.at[other], r.at[other], ssem.at[other], rsem.at[other], *to).wait_recv()
                return c
            copy = remote(s.at[other], r.at[me], ssem.at[other], rsem.at[me], *to)
            if start == "start":
                copy.start()
            else:
                copy.wait_send()
            return c

        lax.fori_loop(1, n, step, 0)

    exch_a = functools.partial(exchange, "x", nx, s_a, r_a, as_sem, ar_sem)
    exch_b = functools.partial(exchange, "y", ny, s_b, r_b, bs_sem, br_sem)
    exch_c = functools.partial(exchange, "y", ny, s_c, r_c, cs_sem, cr_sem)
    exch_d = functools.partial(exchange, "x", nx, s_d, r_d, ds_sem, dr_sem)
    exch_a("start")

    send_y(2)
    send_y(3)
    send_y(4)
    send_y(5)
    build_op(1)

    n_i, n_j = iota((256, 256), 0), iota((256, 256), 1)
    turned = (n_i % 16) // 2 * 32 + n_i // 16 * 2 + n_i % 2
    turn = jnp.where(n_j == turned, 1.0, 0.0).astype(BF)
    back = jnp.where(n_j == n_i % 32 // 2 * 16 + n_i // 32 * 2 + n_i % 2, 1.0, 0.0).astype(BF)
    exch_a("recv")
    rows = dot(turn, r_a[...].reshape(256, 256)).astype(BF)
    for k in range(ny):
        s_b[k] = rows[k * 16:(k + 1) * 16, :]
    r_b[iy] = s_b[iy]
    exch_b("start")

    build_op(2)
    build_op(3)

    ro_f = ro[...].astype(F32)
    ro_cols = jnp.concatenate([ro_f, jnp.zeros((103, 128), F32)], axis=0).T
    lane128 = iota((128, 128), 1)
    coef[...] = jnp.zeros((128, 128), F32)

    def forward(c):
        for copy in y_copies(c):
            copy.wait_recv()
        lo, hi = CHUNKS[c]
        total = coef[...]
        for m in range(lo, hi):
            y = dot(op[m, :, 0:128], irr[m]) + dot(op[m, :, 128:384], ghost[m])
            y = y.astype(BF)
            y_st[m] = y
            g = dot(y, w[degree_of(m)])
            g_st[m] = g
            if m == 0:
                gate[...] = jax.nn.sigmoid(g)
            updated = (irr[m].astype(F32) + gate[...] * g).astype(BF)
            total = total + dot(updated, jnp.where(lane128 == m, ro_cols, 0.0).astype(BF))
        coef[...] = total

    def backward(c):
        lo, hi = CHUNKS[c]
        total = gate_grad[...]
        ag = atom_grad[...]
        for m in range(lo, hi):
            gu = ag[:, m:m + 1] * ro_f[m:m + 1, :]
            total = total + gu * g_st[m]
            if m > 0:
                gg_st[m] = (gu * gate[...]).astype(BF)
        gate_grad[...] = total

    def weight_grad(l):
        lo, hi = l * l, (l + 1) * (l + 1)
        n = (hi - lo) * 128
        part = dot_tn(y_st[lo:hi].reshape(n, 128), gg_st[lo:hi].reshape(n, 128)).astype(BF)
        for k in range(nx):
            gw_send[l, k] = part[k * 16:(k + 1) * 16, :]
        gw_recv[l, ix] = gw_send[l, ix]
        exchange("x", nx, gw_send.at[l], gw_recv.at[l], ws_sem.at[l], wr_sem.at[l], "start")

    forward(0)
    build_op(4)
    build_op(5)
    forward(1)

    exch_b("recv")
    incoming = r_b[...].reshape(256, 256)
    ids = incoming[:, 128:256].astype(F32)[:, 72:73]
    owner = jnp.where(ids == iota((256, 128), 1).astype(F32), 1.0, 0.0)
    own_hot[...] = owner.astype(BF)
    owner_t = jnp.concatenate([owner[0:128, :].T[0:16, :], owner[128:256, :].T[0:16, :]], axis=1).astype(BF)
    block_grad = dot(owner_t, incoming)
    for j in range(8):
        moved = block_grad if j == 0 else pltpu.roll(block_grad, 256 - 25 * j, 1)
        atom_grad[pl.ds(j, 16, stride=8), :] = moved[:, 0:128]
    gate_grad[...] = jnp.zeros((128, 128), F32)

    backward(0)
    backward(1)
    weight_grad(1)
    forward(2)
    backward(2)
    weight_grad(4)
    forward(3)
    backward(3)
    forward(4)
    backward(4)
    weight_grad(3)
    forward(5)

    coef_rows = jnp.zeros((16, 256), F32)
    valid = jnp.where(iota((16, 256), 1) < 25, 1.0, 0.0)
    for j in range(8):
        part = jnp.concatenate([coef[pl.ds(j, 16, stride=8), :], jnp.zeros((16, 128), F32)], axis=1) * valid
        coef_rows = coef_rows + (part if j == 0 else pltpu.roll(part, 25 * j, 1))
    coef_pad = jnp.concatenate([coef_rows, jnp.zeros((112, 256), F32)], axis=0).astype(BF)
    answer = dot(own_hot[...], coef_pad).astype(BF)
    for k in range(ny):
        s_c[k] = answer[k * 16:(k + 1) * 16, :]
    r_c[iy] = s_c[iy]
    exch_c("start")

    backward(5)
    weight_grad(2)
    gu = atom_grad[:, 0:1] * ro_f[0:1, :]
    s = gate[...]
    gg_st[0] = (gu * s + gate_grad[...] * s * (1.0 - s)).astype(BF)
    weight_grad(0)

    exch_c("recv")
    rows = dot(back, r_c[...].reshape(256, 256)).astype(BF)
    for k in range(nx):
        s_d[k] = rows[k * 32:(k + 1) * 32, :]
    r_d[ix] = s_d[ix]
    exch_d("start")

    for l in range(DEGREES):
        exchange("x", nx, gw_send.at[l], gw_recv.at[l], ws_sem.at[l], wr_sem.at[l], "recv")
    for l in range(DEGREES):
        total = gw_recv[l, 0].astype(F32)
        for k in range(1, nx):
            total = total + gw_recv[l, k].astype(F32)
        sum_x_send[l * 16:(l + 1) * 16, :] = total.astype(BF)
    sum_x[yr] = sum_x_send[...]

    def step_u(d, mode):
        other = (yr + d) % 4
        to = yq * 4 + other
        if mode == "recv":
            remote(sum_x_send, sum_x.at[other], us_sem.at[other], ur_sem.at[other], ix, to).wait_recv()
            return
        copy = remote(sum_x_send, sum_x.at[yr], us_sem.at[other], ur_sem.at[yr], ix, to)
        copy.start() if mode == "start" else copy.wait_send()

    def step_v(d, mode):
        other = (yq + d) % 4
        to = other * 4 + yr
        if mode == "recv":
            remote(sum_x_send, sum_y.at[other], vs_sem.at[other], vr_sem.at[other], ix, to).wait_recv()
            return
        copy = remote(sum_y.at[yq], sum_y.at[yq], vs_sem.at[other], vr_sem.at[yq], ix, to)
        copy.start() if mode == "start" else copy.wait_send()

    def step_o(d, mode):
        other = (ix + d) % nx
        if mode == "recv":
            remote(sum_x_send, out_recv.at[other], os_sem.at[other], or_sem.at[other], other, iy).wait_recv()
            return
        copy = remote(out_recv.at[ix], out_recv.at[ix], os_sem.at[other], or_sem.at[ix], other, iy)
        copy.start() if mode == "start" else copy.wait_send()

    for d in range(1, 4):
        step_u(d, "start")

    exch_d("recv")
    fetched = dot(pick_p[...], r_d[...].reshape(256, 256)).astype(BF)
    keep = jnp.where(iota((16, 256), 0) % 4 == iota((16, 256), 1) // 64, 1.0, 0.0)
    for q in range(8):
        rows16 = fetched[q * 16:(q + 1) * 16, 0:200]
        for r in range(4):
            t = q * 4 + r
            out = dot(rows16, basis[t])
            wanted = keep * jnp.where(iota((16, 256), 0) // 4 == r, 1.0, 0.0)
            dens[t:t + 1, :] = jnp.sum(out * wanted, axis=0, keepdims=True)

    for d in range(1, 4):
        step_u(d, "recv")
    total = sum_x[0].astype(F32)
    for k in range(1, 4):
        total = total + sum_x[k].astype(F32)
    sum_y[yq] = total.astype(BF)
    for d in range(1, 4):
        step_v(d, "start")

    folded = dens[:, 0:128] + dens[:, 128:256]
    tmp256[0:32, :] = folded + pltpu.roll(folded, 64, 1)
    even = tmp256[pl.ds(0, 16, stride=2), :]
    odd_rows = tmp256[pl.ds(1, 16, stride=2), :]
    dens_out[...] = jnp.where(iota((16, 128), 1) < 64, even, odd_rows)

    for d in range(1, 4):
        step_v(d, "recv")
    total = sum_y[0].astype(F32)
    for k in range(1, 4):
        total = total + sum_y[k].astype(F32)
    out_recv[ix] = total.astype(BF)
    for d in range(1, nx):
        step_o(d, "start")
    for d in range(1, nx):
        step_o(d, "recv")
    for l in range(DEGREES):
        for k in range(nx):
            gw_out[l, k * 16:(k + 1) * 16, :] = out_recv[k, l * 16:(l + 1) * 16, :].astype(F32)

    for c in range(len(CHUNKS)):
        for copy in x_copies(c) + y_copies(c):
            copy.wait_send()
    for exch in (exch_a, exch_b, exch_c, exch_d):
        exch("send")
    for l in range(DEGREES):
        exchange("x", nx, gw_send.at[l], gw_recv.at[l], ws_sem.at[l], wr_sem.at[l], "send")
    for d in range(1, 4):
        step_u(d, "send")
        step_v(d, "send")
    for d in range(1, nx):
        step_o(d, "send")


def body(nx, ny, irreps, mix_weight, readout, ghost_x, ghost_y, edge_source_row, edge_dst, radial,
         tile_peer, tile_block, tile_count, basis, density_cot):
    irr = jnp.transpose(irreps[0, 0], (1, 0, 2))
    small = jnp.concatenate(
        [
            ghost_x.reshape(1, 128),
            ghost_y.reshape(1, 128),
            tile_peer.reshape(1, 128),
            tile_block.reshape(1, 128),
            jnp.broadcast_to(tile_count.reshape(32, 1), (32, 4)).reshape(1, 128),
            jnp.zeros((3, 128), jnp.int32),
        ],
        axis=0,
    )
    nch = len(CHUNKS)
    dma = pltpu.SemaphoreType.DMA
    vm = pltpu.VMEM
    dens, gw = pl.pallas_call(
        functools.partial(kernel, nx, ny),
        out_shape=(
            jax.ShapeDtypeStruct((16, 128), F32),
            jax.ShapeDtypeStruct((5, 128, 128), F32),
        ),
        in_specs=[pl.BlockSpec(memory_space=pltpu.VMEM)] * 8 + [pl.BlockSpec(memory_space=pl.ANY)],
        out_specs=(pl.BlockSpec(memory_space=pltpu.VMEM),) * 2,
        scratch_shapes=[
            vm((32, 200, 256), BF),
            vm((25, 256, 128), BF),
            vm((25, 128, 128), BF),
            vm((25, 128, 128), BF),
            vm((128, 128), BF),
            vm((128, 256), BF),
            vm((2048, 384), BF),
            vm((128, 2048), BF),
            vm((640, 2048), BF),
            vm((25, 128, 384), BF),
            vm((25, 128, 128), BF),
            vm((25, 128, 128), F32),
            vm((25, 128, 128), BF),
            vm((128, 128), F32),
            vm((128, 128), F32),
            vm((128, 128), F32),
            vm((128, 128), F32),
            vm((256, 128), F32),
            vm((nx, 32, 256), BF), vm((nx, 32, 256), BF),
            vm((ny, 16, 256), BF), vm((ny, 16, 256), BF),
            vm((ny, 16, 256), BF), vm((ny, 16, 256), BF),
            vm((nx, 32, 256), BF), vm((nx, 32, 256), BF),
            vm((128, 256), BF),
            vm((256, 128), BF),
            vm((32, 256), F32),
            vm((5, nx, 16, 128), BF),
            vm((5, nx, 16, 128), BF),
            vm((80, 128), BF),
            vm((4, 80, 128), BF),
            vm((4, 80, 128), BF),
            vm((nx, 80, 128), BF),
            dma,
            dma((nch, 2)), dma((nch, 2)), dma((nch, 2)), dma((nch, 2)),
            dma((nx,)), dma((nx,)), dma((ny,)), dma((ny,)),
            dma((ny,)), dma((ny,)), dma((nx,)), dma((nx,)),
            dma((5, nx)), dma((5, nx)), dma((4,)), dma((4,)), dma((4,)), dma((4,)), dma((nx,)), dma((nx,)),
        ],
        compiler_params=pltpu.CompilerParams(
            collective_id=0, has_side_effects=True, vmem_limit_bytes=48 * 1024 * 1024
        ),
    )(
        irr,
        mix_weight,
        readout,
        small,
        edge_source_row.reshape(16, 128),
        edge_dst.reshape(16, 128),
        radial.reshape(25, 1, 2048),
        density_cot.reshape(16, 128),
        basis.reshape(32, 200, 256),
    )
    return dens.reshape(1, 1, 2048), gw


def solution(mesh):
    nx, ny = mesh.shape["gx"], mesh.shape["gy"]
    placed = (
        P("gx", "gy", None, None, None),
        P(),
        P(),
        P("gx", "gy", None, None),
        P("gx", "gy", None, None),
        P("gx", "gy", None),
        P("gx", "gy", None),
        P("gx", "gy", None, None),
        P("gx", "gy", None, None),
        P("gx", "gy", None, None),
        P("gx", "gy", None),
        P("gx", "gy", None, None, None),
        P("gx", "gy", None),
    )
    return jax.shard_map(
        functools.partial(body, nx, ny),
        mesh=mesh, in_specs=placed, out_specs=(P("gx", "gy", None), P()), check_vma=False,
    )
```

profile of v0, /device:TPU:1, one launch (start us, length us, event | category | flops | bytes accessed | tf_op | source)
XLA Modules:
  0.0 72.9 jit_solution(13555287040249408973)
XLA Ops:
  0.6 0.8 %reshape.39 = s32[1,128]{1,0:T(1,128)S(1)} reshape(s32[1,1,2,64]{3,2,1,0:T(2,128)} %param.16) | data formatting | bytes 1024 | tf_op jit(solution)/shard_map/reshape | solution.py:424
  1.4 0.8 %reshape.40 = s32[1,128]{1,0:T(1,128)S(1)} reshape(s32[1,1,2,64]{3,2,1,0:T(2,128)} %param.17) | data formatting | bytes 1024 | tf_op jit(solution)/shard_map/reshape | solution.py:425
  2.1 0.7 reduce
  2.9 0.8 %copy.17 = s32[1,1,32,4]{3,2,1,0:T(8,128)S(1)} copy(s32[1,1,32,4]{2,3,1,0:T(4,128)} %param.21) | data formatting | bytes 1024 | tf_op args[8]
  3.6 0.1 reshape.41
  3.7 0.8 %copy.18 = s32[1,1,32,4]{3,2,1,0:T(8,128)S(1)} copy(s32[1,1,32,4]{2,3,1,0:T(4,128)} %param.22) | data formatting | bytes 1024 | tf_op args[9]
  4.5 0.1 reshape.42
  4.6 0.7 broadcast_in_dim.11
  5.3 0.1 reshape.43
  5.5 0.0 copy-start
  5.5 1.9 %copy-done = bf16[1,1,32,200,256]{4,3,2,1,0:T(8,128)(2,1)S(1)} copy-done((bf16[1,1,32,200,256]{4,3,2,1,0:T(8,128)(2,1)S(1)}, bf16[1,1,32,200,256]{4,3,2,1,0:T(8,128)(2,1)}, u32[]{:S(2)}) %copy-start) | copy-done | bytes 3276824
  7.4 0.0 copy-start.1
  7.4 1.1 %copy-done.1 = bf16[1,1,128,25,128]{4,2,3,1,0:T(8,128)(2,1)S(1)} copy-done((bf16[1,1,128,25,128]{4,2,3,1,0:T(8,128)(2,1)S(1)}, bf16[1,1,128,25,128]{4,2,3,1,0:T(8,128)(2,1)}, u32[]{:S(2)}) %copy-start.1) | copy-done | bytes 819224
  8.6 0.0 copy-start.2
  8.6 0.9 %copy-done.2 = f32[1,1,25,2048]{3,1,2,0:T(1,128)S(1)} copy-done((f32[1,1,25,2048]{3,1,2,0:T(1,128)S(1)}, f32[1,1,25,2048]{3,1,2,0:T(1,128)}, u32[]{:S(2)}) %copy-start.2) | copy-done | bytes 204824
  9.5 0.0 copy-start.3
  9.5 0.9 %copy-done.3 = bf16[5,128,128]{2,1,0:T(8,128)(2,1)S(1)} copy-done((bf16[5,128,128]{2,1,0:T(8,128)(2,1)S(1)}, bf16[5,128,128]{2,1,0:T(8,128)(2,1)}, u32[]{:S(2)}) %copy-start.3) | copy-done | bytes 163864
  10.4 0.0 copy-start.4
  10.4 0.7 copy-done.4
  11.1 0.7 copy-done.5
  11.8 0.7 copy-done.6
  12.5 59.1 %shard_map.140 = (f32[16,128]{1,0:T(8,128)S(1)}, f32[5,128,128]{2,1,0:T(8,128)S(1)}) custom-call(bf16[25,128,128]{2,1,0:T(8,128)(2,1)S(1)} %bitcast.15, bf16[5,128,128]{2,1,0:T(8,128)(2,1)S(1)} %copy-done.3, bf16[25,128]{1,0:T(8,128)(2,1)S(1)} %copy-done.4, s32[8,128]{1,0:T(8,128)S(1)} %concatenate.3.small, s32[16,128]{1,0:T(8,128)S(1)} %bitcast.18, ...), custom_call_target="tpu_custom_call" | custom-call | tf_op jit(solution)/shard_map/pallas_call | solution.py:436
  71.6 0.6 copy.21
  72.2 0.7 copy.22
  (4 shorter events, 0.0 us)
Async XLA Ops:
  5.5 1.9 %copy-start = (bf16[1,1,32,200,256]{4,3,2,1,0:T(8,128)(2,1)S(1)}, bf16[1,1,32,200,256]{4,3,2,1,0:T(8,128)(2,1)}, u32[]{:S(2)}) copy-start(bf16[1,1,32,200,256]{4,3,2,1,0:T(8,128)(2,1)} %param.24) | copy-start | bytes 9830404
  7.4 1.1 %copy-start.1 = (bf16[1,1,128,25,128]{4,2,3,1,0:T(8,128)(2,1)S(1)}, bf16[1,1,128,25,128]{4,2,3,1,0:T(8,128)(2,1)}, u32[]{:S(2)}) copy-start(bf16[1,1,128,25,128]{4,2,3,1,0:T(8,128)(2,1)} %param.13) | copy-start | bytes 2457604
  8.6 0.9 %copy-start.2 = (f32[1,1,25,2048]{3,1,2,0:T(1,128)S(1)}, f32[1,1,25,2048]{3,1,2,0:T(1,128)}, u32[]{:S(2)}) copy-start(f32[1,1,25,2048]{3,1,2,0:T(1,128)} %param.20) | copy-start | bytes 614404
  9.5 0.9 %copy-start.3 = (bf16[5,128,128]{2,1,0:T(8,128)(2,1)S(1)}, bf16[5,128,128]{2,1,0:T(8,128)(2,1)}, u32[]{:S(2)}) copy-start(bf16[5,128,128]{2,1,0:T(8,128)(2,1)} %w.1) | copy-start | bytes 491524
  10.4 0.7 copy-start.4
  11.1 0.7 copy-start.5
  11.8 0.7 copy-start.6
where the time goes:
time: 73.4 us; the launch traced here: 72.9 us
  Pallas kernels  59.1 us (81%)
  local copies, waits for them, and re-layouts  12.4 us (17%)
    pallas_call x1, Pallas kernels, body(): pl.pallas_call(functools.partial(kernel, nx, ny), out_shape=(jax.ShapeDty...  59.1 us
    unnamed x18, local copies, waits for them, and re-layouts  9.85 us

commit v1 on v0

v1 whole, which is shorter than its diff:
```python
import functools

import jax
import jax.numpy as jnp
from jax import lax
from jax.experimental import pallas as pl
from jax.experimental.pallas import tpu as pltpu
from jax.sharding import PartitionSpec as P

MESH = pl.DeviceIdType.MESH
BF = jnp.bfloat16
F32 = jnp.float32

CHUNKS = ((0, 1), (4, 6), (6, 9), (16, 20), (20, 25), (9, 13), (13, 16), (1, 4))
DEGREES = 5


def degree_of(m):
    l = 0
    while (l + 1) * (l + 1) <= m:
        l += 1
    return l


def iota(shape, dim):
    return lax.broadcasted_iota(jnp.int32, shape, dim)


def dot(a, b):
    return jnp.dot(a, b, preferred_element_type=F32)


def dot_nt(a, b):
    return lax.dot_general(a, b, (((1,), (1,)), ((), ())), preferred_element_type=F32)


def dot_tn(a, b):
    return lax.dot_general(a, b, (((0,), (0,)), ((), ())), preferred_element_type=F32)


def kernel(
    nx, ny,
    irr_h, w_h, ro_h, gx_h, gy_h, src_h, dst_h, rad_h, peer_h, block_h, count_h, basis_h, cot_h,
    dens_out, gw_out,
    w, ro, gxi, gyi, src, dst, rad, peer, block, count, basis, cot, table, roc, xface, yface, hot_x, hot_y, source_hot, dst_mask, scaled, op,
    y_st, g_st, gg_st, gate, coef, gate_grad, atom_grad, tmp256,
    s_a, r_a, s_b, r_b, s_c, r_c, s_d, r_d, pick_p, own_hot, dens,
    gw_send1, gw_recv1, gw_send2, gw_recv2, sum_y, out_recv,
    in_sem, xs_sem, xr_sem, ys_sem, yr_sem,
    as_sem, ar_sem, bs_sem, br_sem, cs_sem, cr_sem, ds_sem, dr_sem,
    ws_sem, wr_sem, us_sem, ur_sem, os_sem, or_sem,
):
    ix = lax.axis_index("gx")
    iy = lax.axis_index("gy")
    left, right = (ix + nx - 1) % nx, (ix + 1) % nx
    lower, upper = (iy + ny - 1) % ny, (iy + 1) % ny

    local = {}
    for n, (name, held, here) in enumerate((
        ("gxi", gx_h, gxi), ("irr", irr_h, table.at[:, pl.ds(0, 128), :]), ("gyi", gy_h, gyi), ("src", src_h, src), ("dst", dst_h, dst),
        ("rad", rad_h, rad), ("peer", peer_h, peer), ("block", block_h, block), ("count", count_h, count),
        ("cot", cot_h, cot), ("basis", basis_h, basis), ("w", w_h, w), ("ro", ro_h, ro),
    )):
        local[name] = pltpu.make_async_copy(held, here, in_sem.at[n])
        local[name].start()

    def arrive(*names):
        for name in names:
            local[name].wait()

    barrier = pltpu.get_barrier_semaphore()

    def greet_x(d, c):
        pl.semaphore_signal(barrier, inc=1, device_id=((ix + d) % nx, iy), device_id_type=MESH)
        return c

    def greet_y(d, c):
        pl.semaphore_signal(barrier, inc=1, device_id=(ix, (iy + d) % ny), device_id_type=MESH)
        return c

    lax.fori_loop(1, nx, greet_x, 0)
    lax.fori_loop(1, ny, greet_y, 0)

    def remote(s, d, ssem, rsem, i, j):
        return pltpu.make_async_remote_copy(
            src_ref=s, dst_ref=d, send_sem=ssem, recv_sem=rsem, device_id=(i, j), device_id_type=MESH
        )

    def x_copies(c):
        lo, hi = CHUNKS[c]
        n = hi - lo
        return (
            remote(xface.at[pl.ds(lo, n), pl.ds(64, 64), :], table.at[pl.ds(lo, n), pl.ds(128, 64), :],
                   xs_sem.at[c, 0], xr_sem.at[c, 0], right, iy),
            remote(xface.at[pl.ds(lo, n), pl.ds(0, 64), :], table.at[pl.ds(lo, n), pl.ds(192, 64), :],
                   xs_sem.at[c, 1], xr_sem.at[c, 1], left, iy),
        )

    def y_copies(c):
        lo, hi = CHUNKS[c]
        n = hi - lo
        return (
            remote(yface.at[pl.ds(lo, n), pl.ds(64, 64), :], table.at[pl.ds(lo, n), pl.ds(256, 64), :],
                   ys_sem.at[c, 0], yr_sem.at[c, 0], ix, upper),
            remote(yface.at[pl.ds(lo, n), pl.ds(0, 64), :], table.at[pl.ds(lo, n), pl.ds(320, 64), :],
                   ys_sem.at[c, 1], yr_sem.at[c, 1], ix, lower),
        )

    def ghost_row(ref):
        return jnp.concatenate([ref[0:1, :], ref[1:2, :]], axis=1)

    arrive("gxi")
    hot_x[...] = jnp.where(iota((128, 128), 0) == ghost_row(gxi), 1.0, 0.0).T.astype(BF)
    arrive("irr")

    chooser = hot_x[...]
    for lo, hi in CHUNKS:
        for m in range(lo, hi):
            xface[m] = dot(chooser, table[m, 0:128, :]).astype(BF)

    arrive("gyi")
    gy_row = ghost_row(gyi)
    for half in range(2):
        hot_y[:, half * 128:(half + 1) * 128] = (
            jnp.where(iota((128, 128), 0) + half * 128 == gy_row, 1.0, 0.0).T.astype(BF)
        )

    def send_y(c):
        for copy in x_copies(c):
            copy.wait_recv()
        lo, hi = CHUNKS[c]
        for m in range(lo, hi):
            yface[m] = dot(hot_y[...], table[m, 0:256, :]).astype(BF)
        for copy in y_copies(c):
            copy.start()

    arrive("src", "dst", "rad")
    src_cols = jnp.concatenate([src[...].astype(F32), jnp.zeros((112, 128), F32)], axis=0).T
    lane384 = iota((128, 384), 1).astype(F32)
    sub128 = iota((128, 128), 0)
    for k in range(16):
        source_hot[k * 128:(k + 1) * 128, :] = jnp.where(src_cols[:, k:k + 1] == lane384, 1.0, 0.0).astype(BF)
        dst_mask[:, k * 128:(k + 1) * 128] = jnp.where(sub128 == dst[k:k + 1, :], 1.0, 0.0).astype(BF)

    def build_op(c):
        lo, hi = CHUNKS[c]
        n = hi - lo
        for i in range(n):
            row = rad[lo + i].astype(BF)
            scaled[i * 128:(i + 1) * 128, :] = dst_mask[...] * jnp.broadcast_to(row, (128, 2048))
        built = dot(scaled[0:n * 128, :], source_hot[...])
        for i in range(n):
            op[lo + i] = built[i * 128:(i + 1) * 128, :].astype(BF)

    arrive("peer", "block", "count", "cot")

    def slot_row(ref):
        return jnp.concatenate([ref[k:k + 1, :] for k in range(4)], axis=1)

    peer_row = slot_row(peer)
    same = (jnp.broadcast_to(peer_row, (128, 128)).astype(F32).T == peer_row.astype(F32)) & (
        iota((128, 128), 0) < iota((128, 128), 1)
    )
    rank = jnp.sum(jnp.where(same, 1.0, 0.0), axis=0, keepdims=True).astype(jnp.int32)
    live_row = (iota((1, 128), 1) // 32) < jnp.concatenate([count[...]] * 4, axis=1)
    position = jnp.where(live_row, peer_row * 2 + rank, -1)
    chosen = jnp.where(iota((256, 128), 0) == position, 1.0, 0.0)
    slot_n = iota((128, 128), 0)
    reorder = jnp.where(iota((128, 128), 1) == slot_n % 4 * 32 + slot_n // 4, 1.0, 0.0).astype(BF)
    for half in range(2):
        pick_p[:, half * 128:(half + 1) * 128] = dot_nt(
            reorder, chosen[half * 128:(half + 1) * 128, :].astype(BF)
        ).astype(BF)
    cot_f = cot[...].astype(F32)
    cot_rows = jnp.concatenate([cot_f[:, u * 128:(u + 1) * 128] for u in range(16)], axis=0).astype(BF)
    tile_n = slot_n % 32
    spread = jnp.where(iota((128, 16), 1) == iota((128, 16), 0) % 32 // 2, 1.0, 0.0).astype(BF)
    picked = dot(spread, cot_rows)
    mine = jnp.where((iota((128, 128), 1) // 64) == tile_n % 2, picked, pltpu.roll(picked, 64, 1))
    both = jnp.concatenate([mine, mine], axis=1)
    weights = jnp.where(iota((128, 256), 1) // 64 == iota((128, 256), 0) // 32, both, 0.0)

    weights_t = jnp.concatenate([weights[:, 0:128].T, weights[:, 128:256].T], axis=0).astype(BF)
    arrive("basis")

    lane_tile = iota((200, 128), 1) % 32

    slot_grad = jnp.zeros((200, 128), F32)
    for t in range(32):
        slot_grad = jnp.where(lane_tile == t, dot(basis[t], weights_t), slot_grad)
    id_rows = jnp.where(iota((56, 128), 0) == 0, jnp.broadcast_to(slot_row(block).astype(F32), (56, 128)), 0.0)
    tmp256[...] = jnp.concatenate([slot_grad, id_rows], axis=0)
    sent = dot_nt(chosen.astype(BF), tmp256[...].astype(BF)).astype(BF)
    for k in range(nx):
        s_a[k] = sent[k * 32:(k + 1) * 32, :]
    r_a[ix] = s_a[ix]

    def exchange(axis, n, s, r, ssem, rsem, mode):
        me = ix if axis == "x" else iy
        if mode != "start":
            to = (right, iy) if axis == "x" else (ix, upper)
            everything = remote(r.at[pl.ds(0, n - 1)], r.at[pl.ds(0, n - 1)], ssem, rsem, *to)
            everything.wait_recv() if mode == "recv" else everything.wait_send()
            return
        for d in range(1, n):
            other = (me + d) % n
            to = (other, iy) if axis == "x" else (ix, other)
            remote(s(other), r.at[me], ssem, rsem, *to).start()

    def slot_of(ref):
        return lambda k: ref.at[k]

    exch_a = functools.partial(exchange, "x", nx, slot_of(s_a), r_a, as_sem.at[0], ar_sem.at[0])
    exch_b = functools.partial(exchange, "y", ny, slot_of(s_b), r_b, bs_sem.at[0], br_sem.at[0])
    exch_c = functools.partial(exchange, "y", ny, slot_of(s_c), r_c, cs_sem.at[0], cr_sem.at[0])
    exch_d = functools.partial(exchange, "x", nx, slot_of(s_d), r_d, ds_sem.at[0], dr_sem.at[0])
    exch_g1 = functools.partial(exchange, "x", nx, slot_of(gw_send1), gw_recv1, ws_sem.at[0], wr_sem.at[0])
    exch_g2 = functools.partial(exchange, "x", nx, slot_of(gw_send2), gw_recv2, ws_sem.at[1], wr_sem.at[1])
    exch_u = functools.partial(exchange, "y", ny, lambda k: sum_y.at[iy], sum_y, us_sem.at[0], ur_sem.at[0])
    exch_o = functools.partial(exchange, "x", nx, lambda k: out_recv.at[ix], out_recv, os_sem.at[0], or_sem.at[0])

    pl.semaphore_wait(barrier, nx + ny - 2)
    for c in range(len(CHUNKS)):
        for copy in x_copies(c):
            copy.start()
    exch_a("start")

    build_op(0)
    build_op(1)
    build_op(2)
    send_y(0)
    send_y(1)
    build_op(3)
    send_y(2)
    send_y(3)
    build_op(4)
    send_y(4)
    send_y(5)
    send_y(6)
    send_y(7)

    n_i, n_j = iota((256, 256), 0), iota((256, 256), 1)
    turned = (n_i % 16) // 2 * 32 + n_i // 16 * 2 + n_i % 2
    turn = jnp.where(n_j == turned, 1.0, 0.0).astype(BF)
    back = jnp.where(n_j == n_i % 32 // 2 * 16 + n_i // 32 * 2 + n_i % 2, 1.0, 0.0).astype(BF)
    exch_a("recv")
    rows = dot(turn, r_a[...].reshape(256, 256)).astype(BF)
    for k in range(ny):
        s_b[k] = rows[k * 16:(k + 1) * 16, :]
    r_b[iy] = s_b[iy]
    exch_b("start")

    build_op(5)
    build_op(6)
    build_op(7)

    arrive("w", "ro")
    ro_f = ro[...].astype(F32)
    ro_cols = jnp.concatenate([ro_f, jnp.zeros((103, 128), F32)], axis=0).T
    lane128 = iota((128, 128), 1)
    coef[...] = jnp.zeros((128, 128), F32)
    for m in range(25):
        roc[m * 128:(m + 1) * 128, :] = jnp.where(lane128 == m, ro_cols, 0.0).astype(BF)

    def forward(c):
        for copy in y_copies(c):
            copy.wait_recv()
        lo, hi = CHUNKS[c]
        ys = [dot(op[m], table[m]).astype(BF) for m in range(lo, hi)]
        gs = [dot(y, w[degree_of(lo + i)]) for i, y in enumerate(ys)]
        if lo == 0:
            gate[...] = jax.nn.sigmoid(gs[0])
        for i, (y, g) in enumerate(zip(ys, gs)):
            y_st[lo + i] = y
            g_st[lo + i] = g
        s = gate[...]
        updated = [(table[lo + i, 0:128, :].astype(F32) + s * g).astype(BF) for i, g in enumerate(gs)]
        wide = updated[0] if len(updated) == 1 else jnp.concatenate(updated, axis=1)
        coef[...] += dot(wide, roc[lo * 128:hi * 128, :])

    def backward(c):
        lo, hi = CHUNKS[c]
        total = gate_grad[...]
        ag = atom_grad[...]
        for m in range(lo, hi):
            gu = ag[:, m:m + 1] * ro_f[m:m + 1, :]
            total = total + gu * g_st[m]
            if m > 0:
                gg_st[m] = (gu * gate[...]).astype(BF)
        gate_grad[...] = total

    def weight_grad(l, held, at):
        lo, hi = l * l, (l + 1) * (l + 1)
        n = (hi - lo) * 128
        part = dot_tn(y_st[lo:hi].reshape(n, 128), gg_st[lo:hi].reshape(n, 128)).astype(BF)
        for k in range(nx):
            held[k, at * 16:(at + 1) * 16, :] = part[k * 16:(k + 1) * 16, :]

    forward(0)
    forward(1)

    exch_b("recv")
    incoming = r_b[...].reshape(256, 256)
    ids = incoming[:, 128:256].astype(F32)[:, 72:73]
    owner = jnp.where(ids == iota((256, 128), 1).astype(F32), 1.0, 0.0)
    own_hot[...] = owner.astype(BF)
    owner_t = jnp.concatenate([owner[0:128, :].T[0:16, :], owner[128:256, :].T[0:16, :]], axis=1).astype(BF)
    block_grad = dot(owner_t, incoming)
    for j in range(8):
        moved = block_grad if j == 0 else pltpu.roll(block_grad, 256 - 25 * j, 1)
        atom_grad[pl.ds(j, 16, stride=8), :] = moved[:, 0:128]
    gate_grad[...] = jnp.zeros((128, 128), F32)

    backward(0)
    backward(1)
    forward(2)
    backward(2)
    weight_grad(2, gw_send1, 0)
    forward(3)
    backward(3)
    forward(4)
    backward(4)
    weight_grad(4, gw_send1, 1)
    forward(5)
    backward(5)
    forward(6)
    backward(6)
    weight_grad(3, gw_send1, 2)
    gw_recv1[ix] = gw_send1[ix]
    exch_g1("start")
    exch_a("send")
    exch_b("send")
    for c in range(len(CHUNKS)):
        for copy in x_copies(c):
            copy.wait_send()
    forward(7)
    backward(7)
    weight_grad(1, gw_send2, 1)
    gu = atom_grad[:, 0:1] * ro_f[0:1, :]
    s = gate[...]
    gg_st[0] = (gu * s + gate_grad[...] * s * (1.0 - s)).astype(BF)
    weight_grad(0, gw_send2, 0)
    gw_recv2[ix] = gw_send2[ix]
    exch_g2("start")

    coef_rows = jnp.zeros((16, 256), F32)
    valid = jnp.where(iota((16, 256), 1) < 25, 1.0, 0.0)
    for j in range(8):
        part = jnp.concatenate([coef[pl.ds(j, 16, stride=8), :], jnp.zeros((16, 128), F32)], axis=1) * valid
        coef_rows = coef_rows + (part if j == 0 else pltpu.roll(part, 25 * j, 1))
    coef_pad = jnp.concatenate([coef_rows, jnp.zeros((112, 256), F32)], axis=0).astype(BF)
    answer = dot(own_hot[...], coef_pad).astype(BF)
    for k in range(ny):
        s_c[k] = answer[k * 16:(k + 1) * 16, :]
    r_c[iy] = s_c[iy]
    exch_c("start")

    def total_of(ref, n):
        total = ref[0].astype(F32)
        for k in range(1, n):
            total = total + ref[k].astype(F32)
        return total

    exch_g1("recv")
    first = total_of(gw_recv1, nx)
    exch_g2("recv")
    second = total_of(gw_recv2, nx)
    sum_y[iy] = jnp.concatenate([second, first], axis=0).astype(BF)
    exch_u("start")

    exch_c("recv")
    rows = dot(back, r_c[...].reshape(256, 256)).astype(BF)
    for k in range(nx):
        s_d[k] = rows[k * 32:(k + 1) * 32, :]
    r_d[ix] = s_d[ix]
    exch_d("start")

    for c in range(len(CHUNKS)):
        for copy in y_copies(c):
            copy.wait_send()
    exch_c("send")
    exch_g1("send")
    exch_g2("send")

    exch_u("recv")
    out_recv[ix] = total_of(sum_y, ny).astype(BF)
    exch_o("start")

    exch_d("recv")
    fetched = dot(pick_p[...], r_d[...].reshape(256, 256)).astype(BF)
    keep = jnp.where(iota((16, 256), 0) % 4 == iota((16, 256), 1) // 64, 1.0, 0.0)
    for q in range(8):
        rows16 = fetched[q * 16:(q + 1) * 16, 0:200]
        for r in range(4):
            t = q * 4 + r
            out = dot(rows16, basis[t])
            wanted = keep * jnp.where(iota((16, 256), 0) // 4 == r, 1.0, 0.0)
            dens[t:t + 1, :] = jnp.sum(out * wanted, axis=0, keepdims=True)
    folded = dens[:, 0:128] + dens[:, 128:256]
    tmp256[0:32, :] = folded + pltpu.roll(folded, 64, 1)
    even = tmp256[pl.ds(0, 16, stride=2), :]
    odd_rows = tmp256[pl.ds(1, 16, stride=2), :]
    dens_out[...] = jnp.where(iota((16, 128), 1) < 64, even, odd_rows)

    exch_d("send")
    exch_u("send")
    exch_o("recv")
    for at, l in enumerate((0, 1, 2, 4, 3)):
        for k in range(nx):
            gw_out[l, k * 16:(k + 1) * 16, :] = out_recv[k, at * 16:(at + 1) * 16, :].astype(F32)
    exch_o("send")


def body(nx, ny, irreps, mix_weight, readout, ghost_x, ghost_y, edge_source_row, edge_dst, radial,
         tile_peer, tile_block, tile_count, basis, density_cot):
    irr = jnp.transpose(irreps[0, 0], (1, 0, 2))
    nch = len(CHUNKS)
    dma = pltpu.SemaphoreType.DMA
    vm = pltpu.VMEM
    dens, gw = pl.pallas_call(
        functools.partial(kernel, nx, ny),
        out_shape=(
            jax.ShapeDtypeStruct((16, 128), F32),
            jax.ShapeDtypeStruct((5, 128, 128), F32),
        ),
        in_specs=[pl.BlockSpec(memory_space=pltpu.HBM)] * 13,
        out_specs=(pl.BlockSpec(memory_space=pltpu.VMEM),) * 2,
        scratch_shapes=[
            vm((5, 128, 128), BF),
            vm((25, 128), BF),
            vm((2, 64), jnp.int32), vm((2, 64), jnp.int32),
            vm((16, 128), jnp.int32), vm((16, 128), jnp.int32),
            vm((25, 1, 2048), F32),
            vm((4, 32), jnp.int32), vm((4, 32), jnp.int32), vm((1, 32), jnp.int32),
            vm((32, 200, 256), BF),
            vm((1, 2048), BF),
            vm((25, 384, 128), BF),
            vm((3200, 128), BF),
            vm((25, 128, 128), BF),
            vm((25, 128, 128), BF),
            vm((128, 128), BF),
            vm((128, 256), BF),
            vm((2048, 384), BF),
            vm((128, 2048), BF),
            vm((640, 2048), BF),
            vm((25, 128, 384), BF),
            vm((25, 128, 128), BF),
            vm((25, 128, 128), F32),
            vm((25, 128, 128), BF),
            vm((128, 128), F32),
            vm((128, 128), F32),
            vm((128, 128), F32),
            vm((128, 128), F32),
            vm((256, 128), F32),
            vm((nx, 32, 256), BF), vm((nx, 32, 256), BF),
            vm((ny, 16, 256), BF), vm((ny, 16, 256), BF),
            vm((ny, 16, 256), BF), vm((ny, 16, 256), BF),
            vm((nx, 32, 256), BF), vm((nx, 32, 256), BF),
            vm((128, 256), BF),
            vm((256, 128), BF),
            vm((32, 256), F32),
            vm((nx, 48, 128), BF), vm((nx, 48, 128), BF),
            vm((nx, 32, 128), BF), vm((nx, 32, 128), BF),
            vm((ny, 80, 128), BF),
            vm((nx, 80, 128), BF),
            dma((13,)),
            dma((nch, 2)), dma((nch, 2)), dma((nch, 2)), dma((nch, 2)),
            dma((1,)), dma((1,)), dma((1,)), dma((1,)), dma((1,)), dma((1,)), dma((1,)), dma((1,)),
            dma((2,)), dma((2,)), dma((1,)), dma((1,)), dma((1,)), dma((1,)),
        ],
        compiler_params=pltpu.CompilerParams(
            collective_id=0, has_side_effects=True, vmem_limit_bytes=60 * 1024 * 1024
        ),
    )(
        irr,
        mix_weight,
        readout,
        ghost_x.reshape(2, 64),
        ghost_y.reshape(2, 64),
        edge_source_row.reshape(16, 128),
        edge_dst.reshape(16, 128),
        radial.reshape(25, 1, 2048),
        jnp.transpose(tile_peer[0, 0]),
        jnp.transpose(tile_block[0, 0]),
        tile_count.reshape(1, 32),
        basis.reshape(32, 200, 256),
        density_cot.reshape(1, 2048),
    )
    return dens.reshape(1, 1, 2048), gw


def solution(mesh):
    nx, ny = mesh.shape["gx"], mesh.shape["gy"]
    placed = (
        P("gx", "gy", None, None, None),
        P(),
        P(),
        P("gx", "gy", None, None),
        P("gx", "gy", None, None),
        P("gx", "gy", None),
        P("gx", "gy", None),
        P("gx", "gy", None, None),
        P("gx", "gy", None, None),
        P("gx", "gy", None, None),
        P("gx", "gy", None),
        P("gx", "gy", None, None, None),
        P("gx", "gy", None),
    )
    return jax.shard_map(
        functools.partial(body, nx, ny),
        mesh=mesh, in_specs=placed, out_specs=(P("gx", "gy", None), P()), check_vma=False,
    )
```

time: 73.4 us -> 49.8 us (0.68)
  Pallas kernels: 59.1 us -> 46 us
  local copies, waits for them, and re-layouts: 12.4 us -> 3.01 us
    pallas_call x1, Pallas kernels: 59.1 us -> 46 us  [body(): pl.pallas_call(functools.partial(kernel, nx, ny), out_shape=(jax.ShapeDty...]
    unnamed x18 -> x2, local copies, waits for them, and re-layouts: 9.85 us -> 3.01 us
    reshape x5 -> x0, local copies, waits for them, and re-layouts: 1.83 us -> none  [the longest x1 0.76 us: body(): ghost_x.reshape(1, 128)]
where the time goes in v1:
time: 49.8 us; the launch traced here: 49.6 us
  Pallas kernels  46 us (92%)
  local copies, waits for them, and re-layouts  3.01 us (6%)
  between operations  0.64 us (1%)
    pallas_call x1, Pallas kernels, body(): pl.pallas_call(functools.partial(kernel, nx, ny), out_shape=(jax.ShapeDty...  46 us
    unnamed x2, local copies, waits for them, and re-layouts  3.01 us

profile of v1, /device:TPU:1, one launch (start us, length us, event | category | flops | bytes accessed | tf_op | source)
XLA Modules:
  0.0 49.6 jit_solution(10834315736453379224)
XLA Ops:
  0.6 46.0 %shard_map.140 = (f32[16,128]{1,0:T(8,128)}, f32[5,128,128]{2,1,0:T(8,128)}) custom-call(bf16[25,128,128]{2,1,0:T(8,128)(2,1)} %bitcast.19, bf16[5,128,128]{2,1,0:T(8,128)(2,1)} %w_h.1, bf16[25,128]{1,0:T(8,128)(2,1)} %ro_h.1, s32[2,64]{1,0:T(2,128)} %bitcast.27, s32[2,64]{1,0:T(2,128)} %bitcast.28, s32[16,128]{1,0:T(8,128)} %bitcast.21, ...), custom_call_target="tpu_custom_call" | custom-call | tf_op jit(solution)/shard_map/pallas_call | solution.py:420
  46.6 1.3 %copy.17 = f32[1,1,2048]{2,1,0:T(1,128)} copy(f32[1,1,2048]{2,1,0:T(1,128)} %bitcast.24) | data formatting | bytes 16384
  47.9 1.7 %copy.18 = f32[5,128,128]{2,1,0:T(8,128)} copy(f32[5,128,128]{2,1,0:T(8,128)} %get-tuple-element.9) | data formatting | bytes 655360

commit v2 on v1

--- a/solution.py
+++ b/solution.py
@@ -41,11 +41,11 @@
 def kernel(
     nx, ny,
     irr_h, w_h, ro_h, gx_h, gy_h, src_h, dst_h, rad_h, peer_h, block_h, count_h, basis_h, cot_h,
-    dens_out, gw_out,
+    dens_out, out_recv2, out_recv1,
     w, ro, gxi, gyi, src, dst, rad, peer, block, count, basis, cot, table, roc, xface, yface, hot_x, hot_y, source_hot, dst_mask, scaled, op,
     y_st, g_st, gg_st, gate, coef, gate_grad, atom_grad, tmp256,
     s_a, r_a, s_b, r_b, s_c, r_c, s_d, r_d, pick_p, own_hot, dens,
-    gw_send1, gw_recv1, gw_send2, gw_recv2, sum_y, out_recv,
+    gw_send1, gw_recv1, gw_send2, gw_recv2, sum_y1, sum_y2,
     in_sem, xs_sem, xr_sem, ys_sem, yr_sem,
     as_sem, ar_sem, bs_sem, br_sem, cs_sem, cr_sem, ds_sem, dr_sem,
     ws_sem, wr_sem, us_sem, ur_sem, os_sem, or_sem,
@@ -216,14 +216,17 @@
     exch_d = functools.partial(exchange, "x", nx, slot_of(s_d), r_d, ds_sem.at[0], dr_sem.at[0])
     exch_g1 = functools.partial(exchange, "x", nx, slot_of(gw_send1), gw_recv1, ws_sem.at[0], wr_sem.at[0])
     exch_g2 = functools.partial(exchange, "x", nx, slot_of(gw_send2), gw_recv2, ws_sem.at[1], wr_sem.at[1])
-    exch_u = functools.partial(exchange, "y", ny, lambda k: sum_y.at[iy], sum_y, us_sem.at[0], ur_sem.at[0])
-    exch_o = functools.partial(exchange, "x", nx, lambda k: out_recv.at[ix], out_recv, os_sem.at[0], or_sem.at[0])
+    exch_u1 = functools.partial(exchange, "y", ny, lambda k: sum_y1.at[iy], sum_y1, us_sem.at[0], ur_sem.at[0])
+    exch_u2 = functools.partial(exchange, "y", ny, lambda k: sum_y2.at[iy], sum_y2, us_sem.at[1], ur_sem.at[1])
+    exch_o1 = functools.partial(exchange, "x", nx, lambda k: out_recv1.at[ix], out_recv1, os_sem.at[0], or_sem.at[0])
+    exch_o2 = functools.partial(exchange, "x", nx, lambda k: out_recv2.at[ix], out_recv2, os_sem.at[1], or_sem.at[1])
 
     pl.semaphore_wait(barrier, nx + ny - 2)
     for c in range(len(CHUNKS)):
         for copy in x_copies(c):
             copy.start()
-    exch_a("start")
+        if c == 2:
+            exch_a("start")
 
     build_op(0)
     build_op(1)
@@ -235,9 +238,6 @@
     send_y(3)
     build_op(4)
     send_y(4)
-    send_y(5)
-    send_y(6)
-    send_y(7)
 
     n_i, n_j = iota((256, 256), 0), iota((256, 256), 1)
     turned = (n_i % 16) // 2 * 32 + n_i // 16 * 2 + n_i % 2
@@ -249,6 +249,10 @@
         s_b[k] = rows[k * 16:(k + 1) * 16, :]
     r_b[iy] = s_b[iy]
     exch_b("start")
+
+    send_y(5)
+    send_y(6)
+    send_y(7)
 
     build_op(5)
     build_op(6)
@@ -298,6 +302,9 @@
 
     forward(0)
     forward(1)
+    forward(2)
+    forward(3)
+    forward(4)
 
     exch_b("recv")
     incoming = r_b[...].reshape(256, 256)
@@ -311,28 +318,22 @@
         atom_grad[pl.ds(j, 16, stride=8), :] = moved[:, 0:128]
     gate_grad[...] = jnp.zeros((128, 128), F32)
 
-    backward(0)
-    backward(1)
-    forward(2)
-    backward(2)
+    for c in range(5):
+        backward(c)
     weight_grad(2, gw_send1, 0)
-    forward(3)
-    backward(3)
-    forward(4)
-    backward(4)
     weight_grad(4, gw_send1, 1)
     forward(5)
     backward(5)
+    exch_a("send")
+    exch_b("send")
+    for c in range(len(CHUNKS)):
+        for copy in x_copies(c):
+            copy.wait_send()
     forward(6)
     backward(6)
     weight_grad(3, gw_send1, 2)
     gw_recv1[ix] = gw_send1[ix]
     exch_g1("start")
-    exch_a("send")
-    exch_b("send")
-    for c in range(len(CHUNKS)):
-        for copy in x_copies(c):
-            copy.wait_send()
     forward(7)
     backward(7)
     weight_grad(1, gw_send2, 1)
@@ -362,11 +363,11 @@
         return total
 
     exch_g1("recv")
-    first = total_of(gw_recv1, nx)
+    sum_y1[iy] = total_of(gw_recv1, nx).astype(BF)
+    exch_u1("start")
     exch_g2("recv")
-    second = total_of(gw_recv2, nx)
-    sum_y[iy] = jnp.concatenate([second, first], axis=0).astype(BF)
-    exch_u("start")
+    sum_y2[iy] = total_of(gw_recv2, nx).astype(BF)
+    exch_u2("start")
 
     exch_c("recv")
     rows = dot(back, r_c[...].reshape(256, 256)).astype(BF)
@@ -382,9 +383,12 @@
     exch_g1("send")
     exch_g2("send")
 
-    exch_u("recv")
-    out_recv[ix] = total_of(sum_y, ny).astype(BF)
-    exch_o("start")
+    exch_u1("recv")
+    out_recv1[ix] = total_of(sum_y1, ny).astype(BF)
+    exch_o1("start")
+    exch_u2("recv")
+    out_recv2[ix] = total_of(sum_y2, ny).astype(BF)
+    exch_o2("start")
 
     exch_d("recv")
     fetched = dot(pick_p[...], r_d[...].reshape(256, 256)).astype(BF)
@@ -403,12 +407,20 @@
     dens_out[...] = jnp.where(iota((16, 128), 1) < 64, even, odd_rows)
 
     exch_d("send")
-    exch_u("send")
-    exch_o("recv")
-    for at, l in enumerate((0, 1, 2, 4, 3)):
-        for k in range(nx):
-            gw_out[l, k * 16:(k + 1) * 16, :] = out_recv[k, at * 16:(at + 1) * 16, :].astype(F32)
-    exch_o("send")
+    exch_u1("send")
+    exch_u2("send")
+    exch_o1("recv")
+    exch_o2("recv")
+    exch_o1("send")
+    exch_o2("send")
+
+
+def spread_kernel(low, high, dens, dens_out, gw_out):
+    dens_out[...] = dens[...]
+    for ref, degrees in ((low, (0, 1)), (high, (2, 4, 3))):
+        for at, l in enumerate(degrees):
+            for k in range(ref.shape[0]):
+                gw_out[l, k * 16:(k + 1) * 16, :] = ref[k, at * 16:(at + 1) * 16, :].astype(F32)
 
 
 def body(nx, ny, irreps, mix_weight, readout, ghost_x, ghost_y, edge_source_row, edge_dst, radial,
@@ -417,14 +429,15 @@
     nch = len(CHUNKS)
     dma = pltpu.SemaphoreType.DMA
     vm = pltpu.VMEM
-    dens, gw = pl.pallas_call(
+    dens, low, high = pl.pallas_call(
         functools.partial(kernel, nx, ny),
         out_shape=(
-            jax.ShapeDtypeStruct((16, 128), F32),
-            jax.ShapeDtypeStruct((5, 128, 128), F32),
+            pltpu.VMEM((16, 128), F32),
+            pltpu.VMEM((nx, 32, 128), BF),
+            pltpu.VMEM((nx, 48, 128), BF),
         ),
         in_specs=[pl.BlockSpec(memory_space=pltpu.HBM)] * 13,
-        out_specs=(pl.BlockSpec(memory_space=pltpu.VMEM),) * 2,
+        out_specs=(pl.BlockSpec(memory_space=pltpu.VMEM),) * 3,
         scratch_shapes=[
             vm((5, 128, 128), BF),
             vm((25, 128), BF),
@@ -461,12 +474,11 @@
             vm((32, 256), F32),
             vm((nx, 48, 128), BF), vm((nx, 48, 128), BF),
             vm((nx, 32, 128), BF), vm((nx, 32, 128), BF),
-            vm((ny, 80, 128), BF),
-            vm((nx, 80, 128), BF),
+            vm((ny, 48, 128), BF), vm((ny, 32, 128), BF),
             dma((13,)),
             dma((nch, 2)), dma((nch, 2)), dma((nch, 2)), dma((nch, 2)),
             dma((1,)), dma((1,)), dma((1,)), dma((1,)), dma((1,)), dma((1,)), dma((1,)), dma((1,)),
-            dma((2,)), dma((2,)), dma((1,)), dma((1,)), dma((1,)), dma((1,)),
+            dma((2,)), dma((2,)), dma((2,)), dma((2,)), dma((2,)), dma((2,)),
         ],
         compiler_params=pltpu.CompilerParams(
             collective_id=0, has_side_effects=True, vmem_limit_bytes=60 * 1024 * 1024
@@ -486,6 +498,14 @@
         basis.reshape(32, 200, 256),
         density_cot.reshape(1, 2048),
     )
+    dens, gw = pl.pallas_call(
+        spread_kernel,
+        out_shape=(
+            jax.ShapeDtypeStruct((16, 128), F32),
+            jax.ShapeDtypeStruct((5, 128, 128), F32),
+        ),
+        compiler_params=pltpu.CompilerParams(vmem_limit_bytes=4 * 1024 * 1024),
+    )(low, high, dens)
     return dens.reshape(1, 1, 2048), gw
 
 

time: 49.8 us -> 43.4 us (0.87)
  Pallas kernels: 46 us -> 42.6 us
  local copies, waits for them, and re-layouts: 3.01 us -> 0 us
    pallas_call x1 -> x2, Pallas kernels: 46 us -> 42.6 us  [the longest x1 41.9 us: body(): pl.pallas_call(functools.partial(kernel, nx, ny), out_shape=(pltpu.VMEM((...]
    unnamed x2 -> x0, local copies, waits for them, and re-layouts: 3.01 us -> none
where the time goes in v2:
time: 43.4 us; the launch traced here: 43.3 us
  Pallas kernels  42.6 us (98%)
  between operations  0.64 us (1%)
    pallas_call x1, Pallas kernels, body(): pl.pallas_call(functools.partial(kernel, nx, ny), out_shape=(pltpu.VMEM((...  41.9 us

profile of v2, /device:TPU:1, one launch (start us, length us, event | category | flops | bytes accessed | tf_op | source)
XLA Modules:
  0.0 43.3 jit_solution(18123434166723947399)
XLA Ops:
  0.6 41.9 %shard_map.140 = (f32[16,128]{1,0:T(8,128)S(1)}, bf16[8,32,128]{2,1,0:T(8,128)(2,1)S(1)}, bf16[8,48,128]{2,1,0:T(8,128)(2,1)S(1)}) custom-call(bf16[25,128,128]{2,1,0:T(8,128)(2,1)} %bitcast.19, bf16[5,128,128]{2,1,0:T(8,128)(2,1)} %w_h.1, bf16[25,128]{1,0:T(8,128)(2,1)} %ro_h.1, s32[2,64]{1,0:T(2,128)} %bitcast.26, s32[2,64]{1,0:T(2,128)} %bitcast.27, ...), custom_call_target="tpu_custom_call" | custom-call | tf_op jit(solution)/shard_map/pallas_call | solution.py:432
  42.5 0.8 %shard_map.141 = (f32[16,128]{1,0:T(8,128)}, f32[5,128,128]{2,1,0:T(8,128)}) custom-call(bf16[8,32,128]{2,1,0:T(8,128)(2,1)S(1)} %get-tuple-element.7.low, bf16[8,48,128]{2,1,0:T(8,128)(2,1)S(1)} %get-tuple-element.8.high, f32[16,128]{1,0:T(8,128)S(1)} %get-tuple-element.9.dens), custom_call_target="tpu_custom_call" | custom-call | tf_op jit(solution)/shard_map/pallas_call | solution.py:501

commit v3 on v2

--- a/solution.py
+++ b/solution.py
@@ -55,6 +55,21 @@
     left, right = (ix + nx - 1) % nx, (ix + 1) % nx
     lower, upper = (iy + ny - 1) % ny, (iy + 1) % ny
 
+    barrier = pltpu.get_barrier_semaphore()
+
+    def hops(d):
+        return min(d, 4 - d)
+
+    z_now, core_now, y_now, x_now = ix // 2, ix % 2, iy // 4, iy % 4
+    x_steps = sorted(((dz, dc) for dz in range(4) for dc in range(2)), key=lambda v: -(2 * hops(v[0]) + v[1]))
+    y_steps = sorted(((dy, dx) for dy in range(4) for dx in range(4)), key=lambda v: -(hops(v[0]) + hops(v[1])))
+    others_x = [(z_now + dz) % 4 * 2 + (core_now + dc) % 2 for dz, dc in x_steps if dz or dc]
+    others_y = [(y_now + dy) % 4 * 4 + (x_now + dx) % 4 for dy, dx in y_steps if dy or dx]
+    for other in others_y:
+        pl.semaphore_signal(barrier, inc=1, device_id=(ix, other), device_id_type=MESH)
+    for other in others_x:
+        pl.semaphore_signal(barrier, inc=1, device_id=(other, iy), device_id_type=MESH)
+
     local = {}
     for n, (name, held, here) in enumerate((
         ("gxi", gx_h, gxi), ("irr", irr_h, table.at[:, pl.ds(0, 128), :]), ("gyi", gy_h, gyi), ("src", src_h, src), ("dst", dst_h, dst),
@@ -68,19 +83,6 @@
         for name in names:
             local[name].wait()
 
-    barrier = pltpu.get_barrier_semaphore()
-
-    def greet_x(d, c):
-        pl.semaphore_signal(barrier, inc=1, device_id=((ix + d) % nx, iy), device_id_type=MESH)
-        return c
-
-    def greet_y(d, c):
-        pl.semaphore_signal(barrier, inc=1, device_id=(ix, (iy + d) % ny), device_id_type=MESH)
-        return c
-
-    lax.fori_loop(1, nx, greet_x, 0)
-    lax.fori_loop(1, ny, greet_y, 0)
-
     def remote(s, d, ssem, rsem, i, j):
         return pltpu.make_async_remote_copy(
             src_ref=s, dst_ref=d, send_sem=ssem, recv_sem=rsem, device_id=(i, j), device_id_type=MESH
@@ -133,14 +135,6 @@
             yface[m] = dot(hot_y[...], table[m, 0:256, :]).astype(BF)
         for copy in y_copies(c):
             copy.start()
-
-    arrive("src", "dst", "rad")
-    src_cols = jnp.concatenate([src[...].astype(F32), jnp.zeros((112, 128), F32)], axis=0).T
-    lane384 = iota((128, 384), 1).astype(F32)
-    sub128 = iota((128, 128), 0)
-    for k in range(16):
-        source_hot[k * 128:(k + 1) * 128, :] = jnp.where(src_cols[:, k:k + 1] == lane384, 1.0, 0.0).astype(BF)
-        dst_mask[:, k * 128:(k + 1) * 128] = jnp.where(sub128 == dst[k:k + 1, :], 1.0, 0.0).astype(BF)
 
     def build_op(c):
         lo, hi = CHUNKS[c]
@@ -202,8 +196,7 @@
             everything = remote(r.at[pl.ds(0, n - 1)], r.at[pl.ds(0, n - 1)], ssem, rsem, *to)
             everything.wait_recv() if mode == "recv" else everything.wait_send()
             return
-        for d in range(1, n):
-            other = (me + d) % n
+        for other in others_x if axis == "x" else others_y:
             to = (other, iy) if axis == "x" else (ix, other)
             remote(s(other), r.at[me], ssem, rsem, *to).start()
 
@@ -222,23 +215,26 @@
     exch_o2 = functools.partial(exchange, "x", nx, lambda k: out_recv2.at[ix], out_recv2, os_sem.at[1], or_sem.at[1])
 
     pl.semaphore_wait(barrier, nx + ny - 2)
+    exch_a("start")
     for c in range(len(CHUNKS)):
         for copy in x_copies(c):
             copy.start()
-        if c == 2:
-            exch_a("start")
+
+    arrive("src", "dst", "rad")
+    src_cols = jnp.concatenate([src[...].astype(F32), jnp.zeros((112, 128), F32)], axis=0).T
+    lane384 = iota((128, 384), 1).astype(F32)
+    sub128 = iota((128, 128), 0)
+    for k in range(16):
+        source_hot[k * 128:(k + 1) * 128, :] = jnp.where(src_cols[:, k:k + 1] == lane384, 1.0, 0.0).astype(BF)
+        dst_mask[:, k * 128:(k + 1) * 128] = jnp.where(sub128 == dst[k:k + 1, :], 1.0, 0.0).astype(BF)
 
     build_op(0)
     build_op(1)
     build_op(2)
+    build_op(3)
     send_y(0)
     send_y(1)
-    build_op(3)
     send_y(2)
-    send_y(3)
-    build_op(4)
-    send_y(4)
-
     n_i, n_j = iota((256, 256), 0), iota((256, 256), 1)
     turned = (n_i % 16) // 2 * 32 + n_i // 16 * 2 + n_i % 2
     turn = jnp.where(n_j == turned, 1.0, 0.0).astype(BF)
@@ -250,6 +246,10 @@
     r_b[iy] = s_b[iy]
     exch_b("start")
 
+    build_op(4)
+    send_y(3)
+    send_y(4)
+
     send_y(5)
     send_y(6)
     send_y(7)
@@ -277,6 +277,11 @@
         for i, (y, g) in enumerate(zip(ys, gs)):
             y_st[lo + i] = y
             g_st[lo + i] = g
+        if c + 1 < len(CHUNKS):
+            coefficients(c, gs)
+
+    def coefficients(c, gs):
+        lo, hi = CHUNKS[c]
         s = gate[...]
         updated = [(table[lo + i, 0:128, :].astype(F32) + s * g).astype(BF) for i, g in enumerate(gs)]
         wide = updated[0] if len(updated) == 1 else jnp.concatenate(updated, axis=1)
@@ -344,6 +349,7 @@
     gw_recv2[ix] = gw_send2[ix]
     exch_g2("start")
 
+    coefficients(7, [g_st[m] for m in range(*CHUNKS[7])])
     coef_rows = jnp.zeros((16, 256), F32)
     valid = jnp.where(iota((16, 256), 1) < 25, 1.0, 0.0)
     for j in range(8):

time: 43.4 us -> 41.9 us (0.965)
  Pallas kernels: 42.6 us -> 41.1 us
    pallas_call x1, Pallas kernels: 41.9 us -> 40.4 us  [body(): pl.pallas_call(functools.partial(kernel, nx, ny), out_shape=(pltpu.VMEM((...]
where the time goes in v3:
time: 41.9 us; the launch traced here: 41.8 us
  Pallas kernels  41.1 us (98%)
  between operations  0.64 us (2%)
    pallas_call x1, Pallas kernels, body(): pl.pallas_call(functools.partial(kernel, nx, ny), out_shape=(pltpu.VMEM((...  40.4 us

profile of v3, /device:TPU:1, one launch (start us, length us, event | category | flops | bytes accessed | tf_op | source)
XLA Modules:
  0.0 41.8 jit_solution(8139393991237224510)
XLA Ops:
  0.6 40.4 %shard_map.140 = (f32[16,128]{1,0:T(8,128)S(1)}, bf16[8,32,128]{2,1,0:T(8,128)(2,1)S(1)}, bf16[8,48,128]{2,1,0:T(8,128)(2,1)S(1)}) custom-call(bf16[25,128,128]{2,1,0:T(8,128)(2,1)} %bitcast.19, bf16[5,128,128]{2,1,0:T(8,128)(2,1)} %w_h.1, bf16[25,128]{1,0:T(8,128)(2,1)} %ro_h.1, s32[2,64]{1,0:T(2,128)} %bitcast.26, s32[2,64]{1,0:T(2,128)} %bitcast.27, ...), custom_call_target="tpu_custom_call" | custom-call | tf_op jit(solution)/shard_map/pallas_call | solution.py:438
  41.0 0.8 %shard_map.141 = (f32[16,128]{1,0:T(8,128)}, f32[5,128,128]{2,1,0:T(8,128)}) custom-call(bf16[8,32,128]{2,1,0:T(8,128)(2,1)S(1)} %get-tuple-element.7.low, bf16[8,48,128]{2,1,0:T(8,128)(2,1)S(1)} %get-tuple-element.8.high, f32[16,128]{1,0:T(8,128)S(1)} %get-tuple-element.9.dens), custom_call_target="tpu_custom_call" | custom-call | tf_op jit(solution)/shard_map/pallas_call | solution.py:507

commit v4 on v3

--- a/solution.py
+++ b/solution.py
@@ -55,6 +55,15 @@
     left, right = (ix + nx - 1) % nx, (ix + 1) % nx
     lower, upper = (iy + ny - 1) % ny, (iy + 1) % ny
 
+    local = {}
+    for n, (name, held, here) in enumerate((
+        ("gxi", gx_h, gxi), ("irr", irr_h, table.at[:, pl.ds(0, 128), :]), ("gyi", gy_h, gyi), ("src", src_h, src), ("dst", dst_h, dst),
+        ("rad", rad_h, rad), ("peer", peer_h, peer), ("block", block_h, block), ("count", count_h, count),
+        ("cot", cot_h, cot), ("basis", basis_h, basis), ("w", w_h, w), ("ro", ro_h, ro),
+    )):
+        local[name] = pltpu.make_async_copy(held, here, in_sem.at[n])
+        local[name].start()
+
     barrier = pltpu.get_barrier_semaphore()
 
     def hops(d):
@@ -69,15 +78,6 @@
         pl.semaphore_signal(barrier, inc=1, device_id=(ix, other), device_id_type=MESH)
     for other in others_x:
         pl.semaphore_signal(barrier, inc=1, device_id=(other, iy), device_id_type=MESH)
-
-    local = {}
-    for n, (name, held, here) in enumerate((
-        ("gxi", gx_h, gxi), ("irr", irr_h, table.at[:, pl.ds(0, 128), :]), ("gyi", gy_h, gyi), ("src", src_h, src), ("dst", dst_h, dst),
-        ("rad", rad_h, rad), ("peer", peer_h, peer), ("block", block_h, block), ("count", count_h, count),
-        ("cot", cot_h, cot), ("basis", basis_h, basis), ("w", w_h, w), ("ro", ro_h, ro),
-    )):
-        local[name] = pltpu.make_async_copy(held, here, in_sem.at[n])
-        local[name].start()
 
     def arrive(*names):
         for name in names:
@@ -308,8 +308,6 @@
     forward(0)
     forward(1)
     forward(2)
-    forward(3)
-    forward(4)
 
     exch_b("recv")
     incoming = r_b[...].reshape(256, 256)
@@ -323,9 +321,13 @@
         atom_grad[pl.ds(j, 16, stride=8), :] = moved[:, 0:128]
     gate_grad[...] = jnp.zeros((128, 128), F32)
 
-    for c in range(5):
+    for c in range(3):
         backward(c)
     weight_grad(2, gw_send1, 0)
+    forward(3)
+    backward(3)
+    forward(4)
+    backward(4)
     weight_grad(4, gw_send1, 1)
     forward(5)
     backward(5)

time: 41.9 us -> 41.7 us (level)
  no operation moved by 1% of the time
where the time goes in v4:
time: 41.7 us; the launch traced here: 41.5 us
  Pallas kernels  40.9 us (98%)
  between operations  0.64 us (2%)
    pallas_call x1, Pallas kernels, body(): pl.pallas_call(functools.partial(kernel, nx, ny), out_shape=(pltpu.VMEM((...  40.2 us

profile of v4, /device:TPU:1, one launch (start us, length us, event | category | flops | bytes accessed | tf_op | source)
XLA Modules:
  0.0 41.5 jit_solution(4252536536571803328)
XLA Ops:
  0.6 40.2 %shard_map.140 = (f32[16,128]{1,0:T(8,128)S(1)}, bf16[8,32,128]{2,1,0:T(8,128)(2,1)S(1)}, bf16[8,48,128]{2,1,0:T(8,128)(2,1)S(1)}) custom-call(bf16[25,128,128]{2,1,0:T(8,128)(2,1)} %bitcast.19, bf16[5,128,128]{2,1,0:T(8,128)(2,1)} %w_h.1, bf16[25,128]{1,0:T(8,128)(2,1)} %ro_h.1, s32[2,64]{1,0:T(2,128)} %bitcast.26, s32[2,64]{1,0:T(2,128)} %bitcast.27, ...), custom_call_target="tpu_custom_call" | custom-call | tf_op jit(solution)/shard_map/pallas_call | solution.py:440
  40.8 0.8 %shard_map.141 = (f32[16,128]{1,0:T(8,128)}, f32[5,128,128]{2,1,0:T(8,128)}) custom-call(bf16[8,32,128]{2,1,0:T(8,128)(2,1)S(1)} %get-tuple-element.7.low, bf16[8,48,128]{2,1,0:T(8,128)(2,1)S(1)} %get-tuple-element.8.high, f32[16,128]{1,0:T(8,128)S(1)} %get-tuple-element.9.dens), custom_call_target="tpu_custom_call" | custom-call | tf_op jit(solution)/shard_map/pallas_call | solution.py:509
